TPU v7x, 32 devices: a whole 2x2x4 slice. The times are simulated.
32 devices in a mesh: dp: 4 (over x, core), fsdp: 8 (over z, y).
Axes of the slice: x: 2, y: 2, z: 4, core: 2. Of those that a mesh axis runs over, the one named last changes fastest.
Arguments:
- tokens: bfloat16 [32768, 1024], P(('dp', 'fsdp')), may hold values from -6 to 6
- first_values: bfloat16 [32768, 1024], P(('dp', 'fsdp')), may hold values from -6 to 6
- lengths: int32 [32], P(('dp', 'fsdp')), may hold values from 256 to 1024, as said below
- cotangent: bfloat16 [32768, 1024], P(('dp', 'fsdp')), may hold values from -6 to 6
- w_query: bfloat16 [1024, 1024], P('dp', 'fsdp'), may hold values from -0.1875 to 0.1875
- w_key: bfloat16 [1024, 1024], P('dp', 'fsdp'), may hold values from -0.1875 to 0.1875
- w_value: bfloat16 [1024, 1024], P('dp', 'fsdp'), may hold values from -0.1875 to 0.1875
- w_out: bfloat16 [1024, 1024], P('dp', 'fsdp'), may hold values from -0.75 to 0.75
- w_gate: bfloat16 [1024, 2816], P('dp', 'fsdp'), may hold values from -0.1875 to 0.1875
- w_up: bfloat16 [1024, 2816], P('dp', 'fsdp'), may hold values from -0.1875 to 0.1875
- w_down: bfloat16 [2816, 1024], P('dp', 'fsdp'), may hold values from -0.109375 to 0.109375
- norm_one: bfloat16 [1024], P('fsdp'), may hold values from 0.5 to 1.5
- norm_two: bfloat16 [1024], P('fsdp'), may hold values from 0.5 to 1.5
Outputs:
- layer_out: bfloat16 [32768, 1024], P(('dp', 'fsdp'))
- input_grad: float32 [32768, 1024], P(('dp', 'fsdp'))
- first_grad: float32 [32768, 1024], P(('dp', 'fsdp'))
- query_grad: float32 [1024, 1024], P('dp', 'fsdp')
- key_grad: float32 [1024, 1024], P('dp', 'fsdp')
- value_grad: float32 [1024, 1024], P('dp', 'fsdp')
- out_grad: float32 [1024, 1024], P('dp', 'fsdp')
- gate_grad: float32 [1024, 2816], P('dp', 'fsdp')
- up_grad: float32 [1024, 2816], P('dp', 'fsdp')
- down_grad: float32 [2816, 1024], P('dp', 'fsdp')
- gain_one_grad: float32 [1024], P('fsdp')
- gain_two_grad: float32 [1024], P('fsdp')
Inputs may be any that keep to these rules, and one draw needn't show every extreme that they name: `lengths`: live tokens of each sequence; slots from there to 1024 are padding. At least one sequence is 1024 long.
All inputs are finite; a program needn't handle non-finite values.
Results may differ from a plain program's by a relative error of at most 0.014.
Values may be sent and summed in bfloat16 or wider, within the bound.
A program may use at most 320 MiB of HBM per device.

v0:
```python
from functools import partial

import jax
import jax.numpy as jnp
from jax import lax
from jax.sharding import PartitionSpec as P

HEADS = 16
HEAD_DIM = 64


def rms_norm(values, gain_vec):
    inverse = lax.rsqrt(jnp.mean(values * values, axis=-1, keepdims=True) + 1e-06)
    return values * inverse * gain_vec


def rotate(values, positions):
    half_dim = values.shape[-1] // 2
    frequency = 10000.0 ** (-jnp.arange(half_dim, dtype=jnp.float32) * 2.0 / values.shape[-1])
    angles = positions[:, None].astype(jnp.float32) * frequency[None, :]
    cosine = jnp.cos(angles)[:, None, :]
    sine_table = jnp.sin(angles)[:, None, :]
    first_half = values[..., :half_dim]
    second_half = values[..., half_dim:]
    return jnp.concatenate(
        [
            first_half * cosine - second_half * sine_table,
            second_half * cosine + first_half * sine_table,
        ],
        axis=-1,
    )


def masked_scores(query_blk, keys_seq, row_start, block_rows):
    scores = (
        jnp.einsum("qhd,khd->hqk", query_blk, keys_seq, preferred_element_type=jnp.float32) * 0.125
    )
    key_pos = jnp.arange(keys_seq.shape[0], dtype=jnp.int32)
    query_pos = row_start + jnp.arange(block_rows, dtype=jnp.int32)
    allowed = key_pos[None, :] <= query_pos[:, None]
    return jnp.where(allowed[None], scores, -1000000000.0)


def attend_forward(query_seq, keys_seq, values_seq, block_rows):
    block_count = query_seq.shape[0] // block_rows

    def one_block(block_index):
        row_start = block_index * block_rows
        query_blk = lax.dynamic_slice_in_dim(query_seq, row_start, block_rows, 0)
        scores = masked_scores(query_blk, keys_seq, row_start, block_rows)
        row_peak = jnp.max(scores, axis=-1, keepdims=True)
        exponent = jnp.exp(scores - row_peak)
        row_total = jnp.sum(exponent, axis=-1, keepdims=True)
        prob_low = (exponent / row_total).astype(jnp.bfloat16)
        attended = jnp.einsum(
            "hqk,khd->qhd", prob_low, values_seq, preferred_element_type=jnp.float32
        )
        return (attended, (row_peak + jnp.log(row_total))[..., 0])

    attended, logsum = lax.map(one_block, jnp.arange(block_count, dtype=jnp.int32))
    return (attended.reshape(query_seq.shape), logsum)


def attend_backward(query_seq, keys_seq, values_seq, grad_seq, logsum, block_rows):
    block_count = query_seq.shape[0] // block_rows

    def one_block(running, block_index):
        key_acc, value_acc = running
        row_start = block_index * block_rows
        query_blk = lax.dynamic_slice_in_dim(query_seq, row_start, block_rows, 0)
        grad_blk = lax.dynamic_slice_in_dim(grad_seq, row_start, block_rows, 0)
        scores = masked_scores(query_blk, keys_seq, row_start, block_rows)
        prob_wide = jnp.exp(scores - logsum[block_index][..., None])
        prob_low = prob_wide.astype(jnp.bfloat16)
        grad_probs = jnp.einsum(
            "qhd,khd->hqk", grad_blk, values_seq, preferred_element_type=jnp.float32
        )
        row_delta = jnp.sum(prob_wide * grad_probs, axis=-1, keepdims=True)
        grad_scores = (0.125 * (prob_wide * (grad_probs - row_delta))).astype(jnp.bfloat16)
        query_part = jnp.einsum(
            "hqk,khd->qhd", grad_scores, keys_seq, preferred_element_type=jnp.float32
        )
        key_acc = key_acc + jnp.einsum(
            "hqk,qhd->khd", grad_scores, query_blk, preferred_element_type=jnp.float32
        )
        value_acc = value_acc + jnp.einsum(
            "hqk,qhd->khd", prob_low, grad_blk, preferred_element_type=jnp.float32
        )
        return ((key_acc, value_acc), query_part)

    zeros_seq = jnp.zeros(query_seq.shape, jnp.float32)
    (key_acc, value_acc), query_parts = lax.scan(
        one_block, (zeros_seq, zeros_seq), jnp.arange(block_count, dtype=jnp.int32)
    )
    return (query_parts.reshape(query_seq.shape), key_acc, value_acc)


def on_device(
    tokens,
    first_values,
    lengths,
    cotangent,
    w_query,
    w_key,
    w_value,
    w_out,
    w_gate,
    w_up,
    w_down,
    norm_one,
    norm_two,
):
    (
        query_part,
        key_part,
        value_part,
        out_part,
        gate_part,
        up_part,
        down_part,
        gain_first,
        gain_second,
    ) = (
        lax.all_gather(w_query, "fsdp", axis=1, tiled=True),
        lax.all_gather(w_key, "fsdp", axis=1, tiled=True),
        lax.all_gather(w_value, "fsdp", axis=1, tiled=True),
        lax.all_gather(w_out, "fsdp", axis=1, tiled=True),
        lax.all_gather(w_gate, "fsdp", axis=1, tiled=True),
        lax.all_gather(w_up, "fsdp", axis=1, tiled=True),
        lax.all_gather(w_down, "fsdp", axis=1, tiled=True),
        lax.all_gather(norm_one, "fsdp", axis=0, tiled=True),
        lax.all_gather(norm_two, "fsdp", axis=0, tiled=True),
    )
    query_full, key_full, value_full, out_full, gate_full, up_full, down_full = (
        lax.all_gather(query_part, "dp", axis=0, tiled=True),
        lax.all_gather(key_part, "dp", axis=0, tiled=True),
        lax.all_gather(value_part, "dp", axis=0, tiled=True),
        lax.all_gather(out_part, "dp", axis=0, tiled=True),
        lax.all_gather(gate_part, "dp", axis=0, tiled=True),
        lax.all_gather(up_part, "dp", axis=0, tiled=True),
        lax.all_gather(down_part, "dp", axis=0, tiled=True),
    )
    gathered = (
        query_full,
        key_full,
        value_full,
        out_full,
        gate_full,
        up_full,
        down_full,
        gain_first,
        gain_second,
    )
    query_w, key_w, value_w, out_w, gate_w, up_w, down_w, gain_first, gain_second = gathered
    gain_one_wide = gain_first.astype(jnp.float32)
    gain_two_wide = gain_second.astype(jnp.float32)
    tok_rows = tokens.shape[0]
    seq_count = lengths.shape[0]
    seq_len = tok_rows // seq_count
    block_rows = min(512, seq_len)
    positions = jnp.arange(seq_len, dtype=jnp.int32)
    row_positions = jnp.tile(positions, seq_count)
    keep_rows = (positions[None, :] < lengths[:, None]).astype(jnp.float32).reshape(tok_rows, 1)

    def by_sequence(array):
        return array.reshape(seq_count, seq_len, HEADS, HEAD_DIM)

    tokens_wide = tokens.astype(jnp.float32)
    normed_low = rms_norm(tokens_wide, gain_one_wide).astype(jnp.bfloat16)
    query_lin = jnp.dot(normed_low, query_w, preferred_element_type=jnp.float32).reshape(
        tok_rows, HEADS, HEAD_DIM
    )
    key_lin = jnp.dot(normed_low, key_w, preferred_element_type=jnp.float32).reshape(
        tok_rows, HEADS, HEAD_DIM
    )
    value_lin = jnp.dot(normed_low, value_w, preferred_element_type=jnp.float32)
    rope_rows = partial(rotate, positions=row_positions)
    query_rot = rope_rows(query_lin).astype(jnp.bfloat16)
    key_rot = rope_rows(key_lin).astype(jnp.bfloat16)
    values_mix = (0.5 * value_lin + 0.5 * first_values.astype(jnp.float32)).astype(jnp.bfloat16)
    attended, logsum = lax.map(
        lambda pieces: attend_forward(pieces[0], pieces[1], pieces[2], block_rows),
        (by_sequence(query_rot), by_sequence(key_rot), by_sequence(values_mix)),
    )
    attended_low = attended.reshape(tok_rows, HEADS * HEAD_DIM).astype(jnp.bfloat16)
    mixed_rows = tokens_wide + jnp.dot(attended_low, out_w, preferred_element_type=jnp.float32)
    second_low = rms_norm(mixed_rows, gain_two_wide).astype(jnp.bfloat16)
    gate_val = jnp.dot(second_low, gate_w, preferred_element_type=jnp.float32)
    up_val = jnp.dot(second_low, up_w, preferred_element_type=jnp.float32)
    hidden = (jax.nn.silu(gate_val) * up_val).astype(jnp.bfloat16)
    ffn_out = jnp.dot(hidden, down_w, preferred_element_type=jnp.float32)
    layer_out = (keep_rows * (mixed_rows + ffn_out)).astype(jnp.bfloat16)
    (
        query_part,
        key_part,
        value_part,
        out_part,
        gate_part,
        up_part,
        down_part,
        gain_first,
        gain_second,
    ) = (
        lax.all_gather(w_query, "fsdp", axis=1, tiled=True),
        lax.all_gather(w_key, "fsdp", axis=1, tiled=True),
        lax.all_gather(w_value, "fsdp", axis=1, tiled=True),
        lax.all_gather(w_out, "fsdp", axis=1, tiled=True),
        lax.all_gather(w_gate, "fsdp", axis=1, tiled=True),
        lax.all_gather(w_up, "fsdp", axis=1, tiled=True),
        lax.all_gather(w_down, "fsdp", axis=1, tiled=True),
        lax.all_gather(norm_one, "fsdp", axis=0, tiled=True),
        lax.all_gather(norm_two, "fsdp", axis=0, tiled=True),
    )
    query_w, key_w, value_w, out_w, gate_w, up_w, down_w = (
        lax.all_gather(query_part, "dp", axis=0, tiled=True),
        lax.all_gather(key_part, "dp", axis=0, tiled=True),
        lax.all_gather(value_part, "dp", axis=0, tiled=True),
        lax.all_gather(out_part, "dp", axis=0, tiled=True),
        lax.all_gather(gate_part, "dp", axis=0, tiled=True),
        lax.all_gather(up_part, "dp", axis=0, tiled=True),
        lax.all_gather(down_part, "dp", axis=0, tiled=True),
    )
    gain_one_wide = gain_first.astype(jnp.float32)
    gain_two_wide = gain_second.astype(jnp.float32)
    grad_top = cotangent.astype(jnp.float32) * keep_rows
    grad_ffn = grad_top.astype(jnp.bfloat16)
    down_sum = jnp.einsum("rf,rd->fd", hidden, grad_ffn, preferred_element_type=jnp.float32)
    grad_hidden = jnp.einsum("rd,fd->rf", grad_ffn, down_w, preferred_element_type=jnp.float32)
    _, swiglu_back = jax.vjp(lambda gate_in, up_in: jax.nn.silu(gate_in) * up_in, gate_val, up_val)
    grad_gate, grad_up = swiglu_back(grad_hidden)
    grad_gate_low = grad_gate.astype(jnp.bfloat16)
    grad_up_low = grad_up.astype(jnp.bfloat16)
    gate_sum = jnp.einsum(
        "rd,rf->df", second_low, grad_gate_low, preferred_element_type=jnp.float32
    )
    up_sum = jnp.einsum("rd,rf->df", second_low, grad_up_low, preferred_element_type=jnp.float32)
    grad_second = jnp.einsum(
        "rf,df->rd", grad_gate_low, gate_w, preferred_element_type=jnp.float32
    ) + jnp.einsum("rf,df->rd", grad_up_low, up_w, preferred_element_type=jnp.float32)
    _, norm_two_back = jax.vjp(rms_norm, mixed_rows, gain_two_wide)
    grad_mixed_norm, gain_two_sum = norm_two_back(grad_second)
    grad_mixed = grad_top + grad_mixed_norm
    grad_branch = grad_mixed.astype(jnp.bfloat16)
    out_sum = jnp.einsum("rd,re->de", attended_low, grad_branch, preferred_element_type=jnp.float32)
    grad_attended = jnp.einsum(
        "re,de->rd", grad_branch, out_w, preferred_element_type=jnp.float32
    ).astype(jnp.bfloat16)
    query_back, key_back, value_back = lax.map(
        lambda pieces: attend_backward(
            pieces[0], pieces[1], pieces[2], pieces[3], pieces[4], block_rows
        ),
        (
            by_sequence(query_rot),
            by_sequence(key_rot),
            by_sequence(values_mix),
            by_sequence(grad_attended),
            logsum,
        ),
    )
    _, rope_back = jax.vjp(rope_rows, query_lin)
    grad_query_low = (
        rope_back(query_back.reshape(tok_rows, HEADS, HEAD_DIM))[0]
        .reshape(tok_rows, HEADS * HEAD_DIM)
        .astype(jnp.bfloat16)
    )
    grad_key_low = (
        rope_back(key_back.reshape(tok_rows, HEADS, HEAD_DIM))[0]
        .reshape(tok_rows, HEADS * HEAD_DIM)
        .astype(jnp.bfloat16)
    )
    value_mix_grad = value_back.reshape(tok_rows, HEADS * HEAD_DIM)
    first_grad = 0.5 * value_mix_grad
    grad_value_low = (0.5 * value_mix_grad).astype(jnp.bfloat16)
    query_sum = jnp.einsum(
        "rd,re->de", normed_low, grad_query_low, preferred_element_type=jnp.float32
    )
    key_sum = jnp.einsum("rd,re->de", normed_low, grad_key_low, preferred_element_type=jnp.float32)
    value_sum = jnp.einsum(
        "rd,re->de", normed_low, grad_value_low, preferred_element_type=jnp.float32
    )
    grad_normed = (
        jnp.einsum("re,de->rd", grad_query_low, query_w, preferred_element_type=jnp.float32)
        + jnp.einsum("re,de->rd", grad_key_low, key_w, preferred_element_type=jnp.float32)
        + jnp.einsum("re,de->rd", grad_value_low, value_w, preferred_element_type=jnp.float32)
    )
    _, norm_one_back = jax.vjp(rms_norm, tokens_wide, gain_one_wide)
    grad_tokens_norm, gain_one_sum = norm_one_back(grad_normed)
    input_grad = grad_mixed + grad_tokens_norm
    (
        query_red,
        key_red,
        value_red,
        out_red,
        gate_red,
        up_red,
        down_red,
        gain_one_red,
        gain_two_red,
    ) = (
        lax.psum_scatter(query_sum, "fsdp", scatter_dimension=1, tiled=True),
        lax.psum_scatter(key_sum, "fsdp", scatter_dimension=1, tiled=True),
        lax.psum_scatter(value_sum, "fsdp", scatter_dimension=1, tiled=True),
        lax.psum_scatter(out_sum, "fsdp", scatter_dimension=1, tiled=True),
        lax.psum_scatter(gate_sum, "fsdp", scatter_dimension=1, tiled=True),
        lax.psum_scatter(up_sum, "fsdp", scatter_dimension=1, tiled=True),
        lax.psum_scatter(down_sum, "fsdp", scatter_dimension=1, tiled=True),
        lax.psum_scatter(gain_one_sum, "fsdp", scatter_dimension=0, tiled=True),
        lax.psum_scatter(gain_two_sum, "fsdp", scatter_dimension=0, tiled=True),
    )
    query_grad, key_grad, value_grad, out_grad, gate_grad, up_grad, down_grad = (
        lax.psum_scatter(query_red, "dp", scatter_dimension=0, tiled=True),
        lax.psum_scatter(key_red, "dp", scatter_dimension=0, tiled=True),
        lax.psum_scatter(value_red, "dp", scatter_dimension=0, tiled=True),
        lax.psum_scatter(out_red, "dp", scatter_dimension=0, tiled=True),
        lax.psum_scatter(gate_red, "dp", scatter_dimension=0, tiled=True),
        lax.psum_scatter(up_red, "dp", scatter_dimension=0, tiled=True),
        lax.psum_scatter(down_red, "dp", scatter_dimension=0, tiled=True),
    )
    gain_one_grad, gain_two_grad = lax.psum((gain_one_red, gain_two_red), "dp")
    return (
        layer_out,
        input_grad,
        first_grad,
        query_grad,
        key_grad,
        value_grad,
        out_grad,
        gate_grad,
        up_grad,
        down_grad,
        gain_one_grad,
        gain_two_grad,
    )


def solution(mesh):
    in_specs = (
        P(("dp", "fsdp"), None),
        P(("dp", "fsdp"), None),
        P(("dp", "fsdp")),
        P(("dp", "fsdp"), None),
        P("dp", "fsdp"),
        P("dp", "fsdp"),
        P("dp", "fsdp"),
        P("dp", "fsdp"),
        P("dp", "fsdp"),
        P("dp", "fsdp"),
        P("dp", "fsdp"),
        P("fsdp"),
        P("fsdp"),
    )
    out_specs = (
        P(("dp", "fsdp"), None),
        P(("dp", "fsdp"), None),
        P(("dp", "fsdp"), None),
        P("dp", "fsdp"),
        P("dp", "fsdp"),
        P("dp", "fsdp"),
        P("dp", "fsdp"),
        P("dp", "fsdp"),
        P("dp", "fsdp"),
        P("dp", "fsdp"),
        P("fsdp"),
        P("fsdp"),
    )
    return jax.shard_map(
        on_device, mesh=mesh, in_specs=in_specs, out_specs=out_specs, check_vma=False
    )
```

profile of v0, /device:TPU:0, one launch (start us, length us, event | category | flops | bytes accessed | tf_op | source)
XLA Modules:
  0.0 2024.8 jit_solution(17395179539060187814)
XLA Ops:
  9.4 32.5 %all_gather.67 = bf16[256,1024]{1,0:T(8,128)(2,1)} all-gather(bf16[256,128]{1,0:T(8,128)(2,1)} %param.22), channel_id=1, replica_groups=mesh['dp'=4,'fsdp'=8] {'fsdp'}, dimensions={1}, use_global_device_ids=true | all-gather | bytes 589824 | tf_op jit(solution)/shard_map/all_gather | solution.py:125
  42.0 30.6 %all_gather.65 = bf16[256,1024]{1,0:T(8,128)(2,1)} all-gather(bf16[256,128]{1,0:T(8,128)(2,1)} %param.21), channel_id=1, replica_groups=mesh['dp'=4,'fsdp'=8] {'fsdp'}, dimensions={1}, use_global_device_ids=true | all-gather | bytes 589824 | tf_op jit(solution)/shard_map/all_gather | solution.py:124
  72.7 30.9 %all_gather.69 = bf16[256,1024]{1,0:T(8,128)(2,1)} all-gather(bf16[256,128]{1,0:T(8,128)(2,1)} %param.23), channel_id=1, replica_groups=mesh['dp'=4,'fsdp'=8] {'fsdp'}, dimensions={1}, use_global_device_ids=true | all-gather | bytes 589824 | tf_op jit(solution)/shard_map/all_gather | solution.py:126
  103.7 31.4 %all_gather.71 = bf16[256,1024]{1,0:T(8,128)(2,1)} all-gather(bf16[256,128]{1,0:T(8,128)(2,1)} %param.24), channel_id=1, replica_groups=mesh['dp'=4,'fsdp'=8] {'fsdp'}, dimensions={1}, use_global_device_ids=true | all-gather | bytes 589824 | tf_op jit(solution)/shard_map/all_gather | solution.py:127
  139.6 16.3 all-gather
  160.5 18.1 all-gather.1
  186.0 6.1 fusion.99
  192.1 15.6 all-gather.13.cloned.1.call-done
  215.4 16.4 all-gather.17.cloned.1.call-done
  231.8 6.9 multiply_convert_fusion.5
  238.7 99.9 %while.47 = (s32[]{:T(128)}, bf16[2,512,16,64]{1,3,2,0:T(8,128)(2,1)}, f32[2,16,512]{2,1,0:T(8,128)}, s32[2]{0:T(128)S(1)}, bf16[1024,16,64]{0,2,1:T(8,128)(2,1)...) while((s32[]{:T(128)}, ...), condition=%wide.region_4.5_spmd, body=%wide.region_1.4_spmd.sunk | while | flops 2248663552 | bytes 135532816 | solution.py:60
  240.5 15.6 fusion.164
  256.1 16.2 fusion.165
  272.3 14.7 bitcast_dynamic-update-slice_fusion.4
  290.0 15.6 fusion.164
  305.5 16.7 fusion.165
  322.3 14.8 bitcast_dynamic-update-slice_fusion.4
  344.2 5.7 multiply_reduce_fusion.3
  353.7 12.6 fusion.103
  366.3 12.2 fusion.104
  378.5 13.8 all-gather.31.cloned.1.call-done
  392.3 21.9 %multiply_convert_fusion.1 = (bf16[1024,2816]{1,0:T(8,128)(2,1)}, bf16[1024,2816]{1,0:T(8,128)(2,1)}, bf16[1024,2816]{1,0:T(8,128)(2,1)}) fusion(f32[1024,2816]{1,0:T(8,128)} %fusion.103, f32[1024,2816]{1,0:T(8,128)} %fusion.104, bf16[2816,1024]{1,0:T(8,128)(2,1)} %all-gather.31.cloned.1.call-done, bf16[1024,1024]{0,1:T(8,128)(2,1)} %copy.55, ...), kind=kOutput, calls=%fused_computation.61 | convolution fusion | flops 5954863104 | bytes 48238592 | tf_op jit(solution)/shard_map/rd,fd->rf/dot_general | solution.py:228
  414.2 10.1 fusion.105
  424.3 13.0 multiply_reduce_fusion.1
  444.5 411.6 %while.48 = (s32[]{:T(128)}, f32[1024,16,64]{0,2,1:T(8,128)}, f32[1024,16,64]{0,2,1:T(8,128)}, f32[2,512,16,64]{1,0,3,2:T(2,128)}, s32[2]{0:T(128)S(1)}, /*index...) while((s32[]{:T(128)}, f32[1024,16,64]{0,2,1:T(8,128)}, ...), condition=%wide.region_9.10_spmd.clone, body=%wide.region_7.9_spmd.clone.sunk | while | flops 5591550464 | bytes 351211840 | solution.py:92
  445.9 17.7 fusion.176
  463.5 13.1 fusion.177
  479.0 56.9 %bitcast_add_fusion.4 = f32[1024,16,64]{0,2,1:T(8,128)} fusion(f32[1024,16,64]{0,2,1:T(8,128)} %get-tuple-element.447, f32[16,512,1024]{2,1,0:T(8,128)} %fusion.176, f32[16,512,1024]{2,1,0:T(8,128)} %fusion.177, f32[16,512]{1,0:T(8,128)S(1)} %dynamic-slice_bitcast_fusion.2, pred[512,1024]{1,0:T(8,128)(4,1)S(1)} %iota_compare_fusion.6, ...), kind=kOutput, calls=%fused_computation.34.clone.1 | convolution fusion | flops 1168122880 | bytes 144769024 | tf_op jit(solution)/shard_map/while/body/eval_jaxpr/while/body/eval_jaxpr/hqk,qhd->khd/dot_general | solution.py:83
  535.9 17.5 bitcast_add_fusion.5
  553.5 52.6 %fusion.178 = f32[1,512,16,64]{1,3,2,0:T(8,128)} fusion(bf16[1024,16,64]{0,2,1:T(8,128)(2,1)S(1)} %get-tuple-element.467, f32[16,512,1024]{2,1,0:T(8,128)} %fusion.176, f32[16,512,1024]{2,1,0:T(8,128)} %fusion.177, f32[16,512]{1,0:T(8,128)S(1)} %dynamic-slice_bitcast_fusion.2, pred[512,1024]{1,0:T(8,128)(4,1)S(1)} %iota_compare_fusion.6), kind=kOutput, calls=%fused_computation.36.clone.1 | convolution fusion | flops 1166025728 | bytes 71860224 | tf_op jit(solution)/shard_map/while/body/eval_jaxpr/while/body/eval_jaxpr/hqk,khd->qhd/dot_general | solution.py:80
  606.1 5.2 copy.85
  611.2 38.0 %dynamic_update_slice.31 = f32[2,512,16,64]{1,0,3,2:T(2,128)} dynamic-update-slice(f32[2,512,16,64]{1,0,3,2:T(2,128)} %get-tuple-element.449, f32[1,512,16,64]{1,0,3,2:T(1,128)} %copy.85, s32[]{:T(128)S(6)} %copy.102, s32[]{:T(128)} %constant.96.clone.1..sunk.1, s32[]{:T(128)} %constant.96.clone.1..sunk.1, s32[]{:T(128)} %constant.96.clone.1..sunk.1) | dynamic-update-slice | bytes 4194308 | tf_op jit(solution)/shard_map/while/body/eval_jaxpr/while/body/jit(dynamic_update_index_in_dim)/dynamic_update_slice | solution.py:60
  650.5 17.7 fusion.176
  668.2 13.1 fusion.177
  683.6 57.5 %bitcast_add_fusion.4 = f32[1024,16,64]{0,2,1:T(8,128)} fusion(f32[1024,16,64]{0,2,1:T(8,128)} %get-tuple-element.447, f32[16,512,1024]{2,1,0:T(8,128)} %fusion.176, f32[16,512,1024]{2,1,0:T(8,128)} %fusion.177, f32[16,512]{1,0:T(8,128)S(1)} %dynamic-slice_bitcast_fusion.2, pred[512,1024]{1,0:T(8,128)(4,1)S(1)} %iota_compare_fusion.6, ...), kind=kOutput, calls=%fused_computation.34.clone.1 | convolution fusion | flops 1168122880 | bytes 144769024 | tf_op jit(solution)/shard_map/while/body/eval_jaxpr/while/body/eval_jaxpr/hqk,qhd->khd/dot_general | solution.py:83
  741.1 18.8 bitcast_add_fusion.5
  759.9 52.6 %fusion.178 = f32[1,512,16,64]{1,3,2,0:T(8,128)} fusion(bf16[1024,16,64]{0,2,1:T(8,128)(2,1)S(1)} %get-tuple-element.467, f32[16,512,1024]{2,1,0:T(8,128)} %fusion.176, f32[16,512,1024]{2,1,0:T(8,128)} %fusion.177, f32[16,512]{1,0:T(8,128)S(1)} %dynamic-slice_bitcast_fusion.2, pred[512,1024]{1,0:T(8,128)(4,1)S(1)} %iota_compare_fusion.6), kind=kOutput, calls=%fused_computation.36.clone.1 | convolution fusion | flops 1166025728 | bytes 71860224 | tf_op jit(solution)/shard_map/while/body/eval_jaxpr/while/body/eval_jaxpr/hqk,khd->qhd/dot_general | solution.py:80
  812.5 5.2 copy.85
  817.7 38.0 %dynamic_update_slice.31 = f32[2,512,16,64]{1,0,3,2:T(2,128)} dynamic-update-slice(f32[2,512,16,64]{1,0,3,2:T(2,128)} %get-tuple-element.449, f32[1,512,16,64]{1,0,3,2:T(1,128)} %copy.85, s32[]{:T(128)S(6)} %copy.102, s32[]{:T(128)} %constant.96.clone.1..sunk.1, s32[]{:T(128)} %constant.96.clone.1..sunk.1, s32[]{:T(128)} %constant.96.clone.1..sunk.1) | dynamic-update-slice | bytes 4194308 | tf_op jit(solution)/shard_map/while/body/eval_jaxpr/while/body/jit(dynamic_update_index_in_dim)/dynamic_update_slice | solution.py:60
  856.1 6.6 reshape.253
  862.7 7.0 multiply_add_fusion.1
  880.4 4.6 fusion.94
  894.0 7.4 fusion.87
  901.5 12.2 fusion.106
  913.8 12.0 fusion.107
  926.5 12.0 fusion.80
  938.6 26.3 %reduce-scatter.15.cloned.1.call-done = f32[1024,128]{1,0:T(8,128)} async-done(((f32[1024,1024]{1,0:T(8,128)}), f32[1024,128]{1,0:T(8,128)}) %reduce-scatter.15.cloned.1.call-update) | async-done | bytes 524304 | tf_op jit(solution)/shard_map/reduce_scatter | solution.py:300
  965.0 92.1 %reduce-scatter.19.cloned.1.call-done = f32[1024,128]{1,0:T(8,128)} async-done(((f32[1024,1024]{1,0:T(8,128)}), f32[1024,128]{1,0:T(8,128)}) %reduce-scatter.19.cloned.1.call-update) | async-done | bytes 524304 | tf_op jit(solution)/shard_map/reduce_scatter | solution.py:301
  1057.1 91.8 %reduce-scatter.23.cloned.1.call-done = f32[1024,128]{1,0:T(8,128)} async-done(((f32[1024,1024]{1,0:T(8,128)}), f32[1024,128]{1,0:T(8,128)}) %reduce-scatter.23.cloned.1.call-update) | async-done | bytes 524304 | tf_op jit(solution)/shard_map/reduce_scatter | solution.py:302
  1149.0 92.1 %reduce-scatter.27.cloned.1.call-done = f32[1024,128]{1,0:T(8,128)} async-done(((f32[1024,1024]{1,0:T(8,128)}), f32[1024,128]{1,0:T(8,128)}) %reduce-scatter.27.cloned.1.call-update) | async-done | bytes 524304 | tf_op jit(solution)/shard_map/reduce_scatter | solution.py:303
  1241.2 195.8 %reduce-scatter.31.cloned.1.call-done = f32[1024,352]{0,1:T(8,128)} async-done(((f32[1024,2816]{0,1:T(8,128)}), f32[1024,352]{0,1:T(8,128)}) %reduce-scatter.31.cloned.1.call-update) | async-done | bytes 1441808 | tf_op jit(solution)/shard_map/reduce_scatter | solution.py:304
  1437.1 195.2 %reduce-scatter.35.cloned.1.call-done = f32[1024,352]{0,1:T(8,128)} async-done(((f32[1024,2816]{0,1:T(8,128)}), f32[1024,352]{0,1:T(8,128)}) %reduce-scatter.35.cloned.1.call-update) | async-done | bytes 1441808 | tf_op jit(solution)/shard_map/reduce_scatter | solution.py:305
  1633.6 5.6 copy.64
  1639.2 12.6 multiply_convert_fusion.3
  1655.7 172.3 %reduce-scatter.39.cloned.1.call-done = f32[2816,128]{1,0:T(8,128)} async-done(((f32[2816,1024]{1,0:T(8,128)}), f32[2816,128]{1,0:T(8,128)}) %reduce-scatter.39.cloned.1.call-update) | async-done | bytes 1441808 | tf_op jit(solution)/shard_map/reduce_scatter | solution.py:306
  1828.1 4.7 fusion.108
  1841.8 5.3 copy.63
  1847.2 19.6 all-reduce.6
  1866.9 6.1 all-reduce.7
  1876.6 24.6 %reduce-scatter.25.cloned.1.call-done = f32[256,128]{1,0:T(8,128)} async-done(((f32[1024,128]{1,0:T(8,128)}), f32[256,128]{1,0:T(8,128)}) %reduce-scatter.25.cloned.1.call-update) | async-done | bytes 131088 | tf_op jit(solution)/shard_map/reduce_scatter | solution.py:313
  1901.2 24.9 %reduce-scatter.29.cloned.1.call-done = f32[256,128]{1,0:T(8,128)} async-done(((f32[1024,128]{1,0:T(8,128)}), f32[256,128]{1,0:T(8,128)}) %reduce-scatter.29.cloned.1.call-update) | async-done | bytes 131088 | tf_op jit(solution)/shard_map/reduce_scatter | solution.py:314
  1926.1 30.5 %reduce-scatter.33.cloned.1.call-done = f32[256,352]{0,1:T(8,128)} async-done(((f32[1024,352]{0,1:T(8,128)}), f32[256,352]{0,1:T(8,128)}) %reduce-scatter.33.cloned.1.call-update) | async-done | bytes 360464 | tf_op jit(solution)/shard_map/reduce_scatter | solution.py:315
  1956.7 30.7 %reduce-scatter.37.cloned.1.call-done = f32[256,352]{0,1:T(8,128)} async-done(((f32[1024,352]{0,1:T(8,128)}), f32[256,352]{0,1:T(8,128)}) %reduce-scatter.37.cloned.1.call-update) | async-done | bytes 360464 | tf_op jit(solution)/shard_map/reduce_scatter | solution.py:316
  1987.4 30.4 %reduce-scatter.41.cloned.1.call-done = f32[704,128]{1,0:T(8,128)} async-done(((f32[2816,128]{1,0:T(8,128)}), f32[704,128]{1,0:T(8,128)}) %reduce-scatter.41.cloned.1.call-update) | async-done | bytes 360464 | tf_op jit(solution)/shard_map/reduce_scatter | solution.py:317
  (200 shorter events, 86.8 us)
Async XLA Ops:
  7.2 128.0 %all-gather.21.cloned.1.call-start = ((), (), s32[]{:S(2)}) async-start(), calls=%async_computation.18 | async-start | bytes 1622016 | tf_op jit(solution)/shard_map/all_gather | solution.py:128
  7.9 128.0 %all-gather.25.cloned.1.call-start = ((), (), s32[]{:S(2)}) async-start(), calls=%async_computation.20 | async-start | bytes 1622016 | tf_op jit(solution)/shard_map/all_gather | solution.py:129
  8.7 176.7 %all-gather.29.cloned.1.call-start = ((), (), s32[]{:S(2)}) async-start(), calls=%async_computation.22 | async-start | bytes 1622016 | tf_op jit(solution)/shard_map/all_gather | solution.py:130
  9.4 176.6 %all-gather.15.cloned.1.call-start = ((), (), s32[]{:S(2)}) async-start(), calls=%async_computation.15 | async-start | bytes 2621440 | tf_op jit(solution)/shard_map/all_gather | solution.py:136
  42.0 165.8 %all-gather.13.cloned.1.call-start = ((), (), s32[]{:S(2)}) async-start(), calls=%async_computation.14 | async-start | bytes 2621440 | tf_op jit(solution)/shard_map/all_gather | solution.py:135
  72.7 159.1 %all-gather.17.cloned.1.call-start = ((), (), s32[]{:S(2)}) async-start(), calls=%async_computation.16 | async-start | bytes 2621440 | tf_op jit(solution)/shard_map/all_gather | solution.py:137
  103.7 35.9 %copy-start.33 = (bf16[128]{0:T(256)(128)(2,1)S(1)}, bf16[128]{0:T(256)(128)(2,1)}, u32[]{:S(2)}) copy-start(bf16[128]{0:T(256)(128)(2,1)} %param.28) | copy-start | bytes 772
  103.7 240.5 %all-gather.19.cloned.1.call-start = ((), (), s32[]{:S(2)}) async-start(), calls=%async_computation.17 | async-start | bytes 2621440 | tf_op jit(solution)/shard_map/all_gather | solution.py:138
  135.1 218.5 %all-gather.23.cloned.1.call-start = ((), (), s32[]{:S(2)}) async-start(), calls=%async_computation.19 | async-start | bytes 7208960 | tf_op jit(solution)/shard_map/all_gather | solution.py:139
  135.9 230.4 %all-gather.27.cloned.1.call-start = ((), (), s32[]{:S(2)}) async-start(), calls=%async_computation.21 | async-start | bytes 7208960 | tf_op jit(solution)/shard_map/all_gather | solution.py:140
  136.6 255.7 %all-gather.31.cloned.1.call-start = ((), (), s32[]{:S(2)}) async-start(), calls=%async_computation.23 | async-start | bytes 7208960 | tf_op jit(solution)/shard_map/all_gather | solution.py:141
  136.7 23.8 %copy-start.34 = (bf16[128]{0:T(256)(128)(2,1)S(1)}, bf16[128]{0:T(256)(128)(2,1)}, u32[]{:S(2)}) copy-start(bf16[128]{0:T(256)(128)(2,1)} %param.29) | copy-start | bytes 772
  139.6 68.1 %copy-start.4 = (bf16[1024,1024]{0,1:T(8,128)(2,1)}, bf16[1024,1024]{0,1:T(8,128)(2,1)S(1)}, u32[]{:S(2)}) copy-start(bf16[1024,1024]{0,1:T(8,128)(2,1)S(1)} %copy.51) | copy-start | bytes 6291460
  155.9 75.9 %copy-start.26 = (f32[8,1,128]{2,1,0:T(1,128)}, f32[8,1,128]{2,1,0:T(1,128)S(1)}, u32[]{:S(2)}) copy-start(f32[8,1,128]{2,1,0:T(1,128)S(1)} %convert_element_type.152) | copy-start | bytes 12292
  184.8 47.0 %copy-start.28 = (f32[1024]{0:T(1024)}, f32[1024]{0:T(1024)S(1)}, u32[]{:S(2)}) copy-start(f32[1024]{0:T(1024)S(1)} %fusion.91) | copy-start | bytes 12292
  185.4 26.7 %copy-start.18 = (f32[1024,32]{0,1:T(8,128)}, f32[1024,32]{0,1:T(8,128)S(1)}, u32[]{:S(2)}) copy-start(f32[1024,32]{0,1:T(8,128)S(1)} %get-tuple-element.282) | copy-start | bytes 393220
  185.4 26.7 %copy-start.20 = (f32[1024,32]{0,1:T(8,128)}, f32[1024,32]{0,1:T(8,128)S(1)}, u32[]{:S(2)}) copy-start(f32[1024,32]{0,1:T(8,128)S(1)} %get-tuple-element.283) | copy-start | bytes 393220
  185.4 779.5 %reduce-scatter.15.cloned.1.call-start = ((), (), s32[]{:S(2)}) async-start(), calls=%async_computation.24 | async-start | bytes 4718592 | tf_op jit(solution)/shard_map/reduce_scatter | solution.py:300
  207.7 4.4 copy-start.11
  256.1 16.2 copy-start
  256.1 16.2 copy-start.16
  287.0 1.3 copy-start.17
  305.5 16.7 copy-start
  305.5 16.7 copy-start.16
  337.0 1.3 copy-start.17
  344.2 7.7 copy-start.23
  349.9 2.0 copy-start.6
  366.3 26.1 %copy-start.30 = (f32[1024]{0:T(1024)S(1)}, f32[1024]{0:T(1024)}, u32[]{:S(2)}) copy-start(f32[1024]{0:T(1024)} %fusion.90) | copy-start | bytes 12292
  414.2 10.1 copy-start.7
  424.3 13.0 copy-start.10
  437.3 3.5 copy-start.36
  440.8 3.7 copy-start.8
  445.9 17.7 copy-start.1
  463.5 15.1 copy-start.22
  650.5 17.7 copy-start.1
  668.2 15.1 copy-start.22
  856.1 6.7 copy-start.19
  856.1 6.7 copy-start.21
  869.7 2.3 copy-start.5
  869.7 2.3 copy-start.27
  869.7 2.3 copy-start.29
  876.4 180.6 %reduce-scatter.19.cloned.1.call-start = ((), (), s32[]{:S(2)}) async-start(), calls=%async_computation.26 | async-start | bytes 4718592 | tf_op jit(solution)/shard_map/reduce_scatter | solution.py:301
  879.1 1.3 copy-start.14
  885.0 263.9 %reduce-scatter.23.cloned.1.call-start = ((), (), s32[]{:S(2)}) async-start(), calls=%async_computation.28 | async-start | bytes 4718592 | tf_op jit(solution)/shard_map/reduce_scatter | solution.py:302
  887.7 1.9 copy-start.2
  894.0 347.1 %reduce-scatter.27.cloned.1.call-start = ((), (), s32[]{:S(2)}) async-start(), calls=%async_computation.30 | async-start | bytes 4718592 | tf_op jit(solution)/shard_map/reduce_scatter | solution.py:303
  901.4 535.6 %reduce-scatter.31.cloned.1.call-start = ((), (), s32[]{:S(2)}) async-start(), calls=%async_computation.32 | async-start | bytes 12976128 | tf_op jit(solution)/shard_map/reduce_scatter | solution.py:304
  913.7 718.6 %reduce-scatter.35.cloned.1.call-start = ((), (), s32[]{:S(2)}) async-start(), calls=%async_computation.34 | async-start | bytes 12976128 | tf_op jit(solution)/shard_map/reduce_scatter | solution.py:305
  925.8 902.2 %reduce-scatter.39.cloned.1.call-start = ((), (), s32[]{:S(2)}) async-start(), calls=%async_computation.36 | async-start | bytes 12976128 | tf_op jit(solution)/shard_map/reduce_scatter | solution.py:306
  938.5 693.8 %copy-start.37 = (u32[32]{0:T(128)S(1)}, u32[32]{0:T(128)}, u32[]{:S(2)}) copy-start(u32[32]{0:T(128)} %constant.116) | copy-start | bytes 388
  938.5 934.5 %reduce-scatter.17.cloned.1.call-start = ((), (), s32[]{:S(2)}) async-start(), calls=%async_computation.25 | async-start | bytes 655360 | tf_op jit(solution)/shard_map/reduce_scatter | solution.py:311
  964.9 911.7 %reduce-scatter.21.cloned.1.call-start = ((), (), s32[]{:S(2)}) async-start(), calls=%async_computation.27 | async-start | bytes 655360 | tf_op jit(solution)/shard_map/reduce_scatter | solution.py:312
  1057.1 844.1 %reduce-scatter.25.cloned.1.call-start = ((), (), s32[]{:S(2)}) async-start(), calls=%async_computation.29 | async-start | bytes 655360 | tf_op jit(solution)/shard_map/reduce_scatter | solution.py:313
  1149.0 777.2 %reduce-scatter.29.cloned.1.call-start = ((), (), s32[]{:S(2)}) async-start(), calls=%async_computation.31 | async-start | bytes 655360 | tf_op jit(solution)/shard_map/reduce_scatter | solution.py:314
  1241.1 715.6 %reduce-scatter.33.cloned.1.call-start = ((), (), s32[]{:S(2)}) async-start(), calls=%async_computation.33 | async-start | bytes 1802240 | tf_op jit(solution)/shard_map/reduce_scatter | solution.py:315
  1437.0 550.4 %reduce-scatter.37.cloned.1.call-start = ((), (), s32[]{:S(2)}) async-start(), calls=%async_computation.35 | async-start | bytes 1802240 | tf_op jit(solution)/shard_map/reduce_scatter | solution.py:316
  1632.3 385.5 %reduce-scatter.41.cloned.1.call-start = ((), (), s32[]{:S(2)}) async-start(), calls=%async_computation.37 | async-start | bytes 1802240 | tf_op jit(solution)/shard_map/reduce_scatter | solution.py:317
  1828.0 4.7 copy-start.15
  1828.1 4.7 copy-start.35
  1832.8 2.4 copy-start.3
  1832.8 2.9 copy-start.12
  1835.7 3.1 copy-start.25
  1835.7 3.1 copy-start.9
  1841.8 5.3 copy-start.32
  (3 other events, 2.6 us)
Sparse Core Ops, SparseCore 0:
  10.2 50.5 all-gather.20
  63.0 50.6 all-gather.24
  115.7 45.6 all-gather.28
  162.8 20.9 all-gather.14
  185.1 22.5 all-gather.12
  209.2 22.5 all-gather.16
  233.3 22.5 all-gather.18
  257.5 44.1 all-gather.22
  303.3 44.1 all-gather.26
  348.9 43.3 all-gather.30
  876.6 88.2 reduce-scatter.14
  968.8 88.1 reduce-scatter.18
  1060.7 88.1 reduce-scatter.22
  1152.9 88.2 reduce-scatter.26
  1244.5 192.4 reduce-scatter.30
  1440.5 191.7 reduce-scatter.34
  1635.7 192.2 reduce-scatter.38
  1830.9 20.7 reduce-scatter.16
  1854.9 21.6 reduce-scatter.20
  1879.5 21.6 reduce-scatter.24
  1904.5 21.6 reduce-scatter.28
  1929.3 27.3 reduce-scatter.32
  1960.0 27.3 reduce-scatter.36
  1990.4 27.3 reduce-scatter.40
where the time goes:
time: 2030 us; the launch traced here: 2020 us
  waiting for transfers between devices  1060 us (52%)
  matrix products  554 us (27%)
  blocking collectives  186 us (9%)
  local copies, waits for them, and re-layouts  138 us (7%)
  other arithmetic  61.9 us (3%)
    reduce_scatter x1, waiting for transfers between devices, on_device(): lax.psum_scatter(gate_sum, 'fsdp', scatter_dimension=1, tiled=True)  196 us
    reduce_scatter x1, waiting for transfers between devices, on_device(): lax.psum_scatter(up_sum, 'fsdp', scatter_dimension=1, tiled=True)  195 us
    reduce_scatter x1, waiting for transfers between devices, on_device(): lax.psum_scatter(down_sum, 'fsdp', scatter_dimension=1, tiled=True)  172 us
    dot_general x2, matrix products, one_block(): jnp.einsum('hqk,qhd->khd', grad_scores, query_blk, preferred_element_type...  114 us
    dot_general x2, matrix products, one_block(): jnp.einsum('hqk,khd->qhd', grad_scores, keys_seq, preferred_element_type=...  105 us
    reduce_scatter x1, waiting for transfers between devices, on_device(): lax.psum_scatter(out_sum, 'fsdp', scatter_dimension=1, tiled=True)  92.1 us
    reduce_scatter x1, waiting for transfers between devices, on_device(): lax.psum_scatter(key_sum, 'fsdp', scatter_dimension=1, tiled=True)  92.1 us
    reduce_scatter x1, waiting for transfers between devices, on_device(): lax.psum_scatter(value_sum, 'fsdp', scatter_dimension=1, tiled=True)  91.8 us
  transfers between devices with their start and end apart: 24, of which 16 were waited for; matrix products, arithmetic and copies ran while one was open for 13% of the time, Pallas kernels for 0%

commit v1 on v0

--- a/solution.py
+++ b/solution.py
@@ -2,7 +2,10 @@
 
 import jax
 import jax.numpy as jnp
+import numpy as np
 from jax import lax
+from jax.experimental import pallas as pl
+from jax.experimental.pallas import tpu as pltpu
 from jax.sharding import PartitionSpec as P
 
 HEADS = 16
@@ -95,7 +98,7 @@
     return (query_parts.reshape(query_seq.shape), key_acc, value_acc)
 
 
-def on_device(
+def on_device_general(
     tokens,
     first_values,
     lengths,
@@ -333,6 +336,483 @@
     )
 
 
+MESH_ID = pl.DeviceIdType.MESH
+BF = jnp.bfloat16
+F32 = jnp.float32
+NN = (((1,), (0,)), ((), ()))
+NT = (((1,), (1,)), ((), ()))
+TN = (((0,), (0,)), ((), ()))
+
+
+def mm(a, b, dims):
+    return lax.dot_general(a, b, dims, preferred_element_type=F32)
+
+
+def place():
+    dp, fs = lax.axis_index("dp"), lax.axis_index("fsdp")
+    return dp // 2, dp % 2, fs // 2, fs % 2
+
+
+def device(x, c, z, y):
+    return (2 * x + c, 2 * z + y)
+
+
+def greet(x, c, z, y):
+    barrier = pltpu.get_barrier_semaphore()
+    peers = [device(1 - x, c, z, y), device(x, 1 - c, z, y), device(x, c, z, 1 - y)]
+    peers += [device(x, c, lax.rem(z + d, 4), y) for d in (1, 2, 3)]
+    for peer in peers:
+        pl.semaphore_signal(barrier, inc=1, device_id=peer, device_id_type=MESH_ID)
+    pl.semaphore_wait(barrier, len(peers))
+
+
+def block(spec, ref, z, y, x, c, half):
+    rows, cols, along = spec
+    size = rows if half is None else rows // 2
+    start = 0 if half is None else half * (rows // 2)
+    dp = 2 * x + c
+    if along == "rows":
+        return ref.at[z, y, pl.ds(pl.multiple_of(dp * rows + start, 16), size)]
+    return ref.at[z, y, pl.ds(start, size), pl.ds(pl.multiple_of(dp * cols, 128), cols)]
+
+
+ALL = slice(None)
+
+
+class Gather:
+    def __init__(self, at, spec, shard, full, send, recv, local, index):
+        self.at, self.spec, self.shard, self.full = at, spec, shard, full
+        self.send, self.recv, self.local, self.index = send, recv, local, index
+        self.copies = {}
+
+    def part(self, z, y, x, c, half):
+        return block(self.spec, self.full, z, y, x, c, half)
+
+    def start(self, slot, source, target, peer):
+        copy = pltpu.make_async_remote_copy(
+            src_ref=source,
+            dst_ref=target,
+            send_sem=self.send.at[self.index, slot],
+            recv_sem=self.recv.at[self.index, slot],
+            device_id=peer,
+            device_id_type=MESH_ID,
+        )
+        copy.start()
+        self.copies[slot] = copy
+
+    def go(self, slot, region, peer):
+        self.start(slot, region, region, peer)
+
+    def arrive(self, *slots):
+        for slot in slots:
+            self.copies[slot].wait_recv()
+
+    def tick0(self):
+        x, c, z, y = self.at
+        own = self.part(z, y, x, c, None)
+        for d in (1, 2, 3):
+            self.start(d - 1, self.shard, own, device(x, c, lax.rem(z + d, 4), y))
+        self.own = pltpu.make_async_copy(self.shard, own, self.local.at[self.index])
+        self.own.start()
+
+    def tick1(self):
+        x, c, z, y = self.at
+        self.own.wait()
+        self.arrive(0, 1, 2)
+        self.go(4, self.part(ALL, y, x, c, 0), device(1 - x, c, z, y))
+        self.go(5, self.part(ALL, y, x, c, 1), device(x, c, z, 1 - y))
+        self.go(3, self.part(ALL, y, x, c, None), device(x, 1 - c, z, y))
+
+    def tick2(self):
+        x, c, z, y = self.at
+        across, beside, other = device(1 - x, c, z, y), device(x, c, z, 1 - y), device(x, 1 - c, z, y)
+        self.arrive(4, 5)
+        self.go(6, self.part(ALL, y, 0, c, 0), beside)
+        self.go(7, self.part(ALL, y, 1, c, 0), beside)
+        self.go(8, self.part(ALL, ALL, x, c, 1), across)
+        self.go(9, self.part(ALL, y, 1 - x, c, 0), other)
+        self.go(10, self.part(ALL, 1 - y, x, c, 1), other)
+
+    def tick3(self):
+        x, c, z, y = self.at
+        other = device(x, 1 - c, z, y)
+        self.arrive(6, 7, 8)
+        self.go(11, self.part(ALL, 1 - y, 0, c, 0), other)
+        self.go(12, self.part(ALL, 1 - y, 1, c, 0), other)
+        self.go(13, self.part(ALL, ALL, 1 - x, c, 1), other)
+
+    def tick4(self):
+        self.arrive(3, 9, 10, 11, 12, 13)
+
+    def finish(self):
+        for copy in self.copies.values():
+            copy.wait_send()
+
+
+QKV, OUT, GATE, UP, DOWN, GAIN = range(6)
+SPECS = {
+    QKV: (256, 384, "rows"),
+    OUT: (256, 128, "rows"),
+    GATE: (352, 256, "cols"),
+    UP: (352, 256, "cols"),
+    DOWN: (704, 128, "rows"),
+    GAIN: (32, 128, "rows"),
+}
+
+
+def full_shape(spec):
+    rows, cols, along = spec
+    return (4, 2, 4 * rows, cols) if along == "rows" else (4, 2, rows, 4 * cols)
+
+
+def turn(u, cosine, low_sine, high_sine):
+    return u * cosine + pltpu.roll(u, 96, 1) * low_sine + pltpu.roll(u, 32, 1) * high_sine
+
+
+def head_mask(shape, head):
+    lane = lax.broadcasted_iota(jnp.int32, shape, 1)
+    return (lane < 64) if head == 0 else (lane >= 64)
+
+
+def attend_pair(q, k, v, blk):
+    rows = q.shape[0]
+    v_turned = v.T
+    out, sums = [], [[], []]
+    key_index = lax.broadcasted_iota(jnp.int32, (blk, blk), 0)
+    query_index = lax.broadcasted_iota(jnp.int32, (blk, blk), 1)
+    allowed = key_index <= query_index
+    for j in range(rows // blk):
+        lo, hi = j * blk, (j + 1) * blk
+        parts = []
+        for head in range(2):
+            qh = jnp.where(head_mask((blk, 128), head), q[lo:hi], 0)
+            s = mm(k[:hi], qh, NT)
+            tail = jnp.where(allowed, s[lo:hi], -1000000000.0)
+            peak = jnp.max(tail, axis=0, keepdims=True)
+            if j:
+                peak = jnp.maximum(peak, jnp.max(s[:lo], axis=0, keepdims=True))
+            e = jnp.exp(tail - peak)
+            total = jnp.sum(e, axis=0, keepdims=True)
+            e = e.astype(BF)
+            if j:
+                head_part = jnp.exp(s[:lo] - peak)
+                total = total + jnp.sum(head_part, axis=0, keepdims=True)
+                e = jnp.concatenate([head_part.astype(BF), e], axis=0)
+            parts.append(mm(v_turned[head * 64 : head * 64 + 64, :hi], e, NN) * (1.0 / total))
+            sums[head].append(peak + jnp.log(total))
+        out.append(jnp.concatenate(parts, axis=0).T.astype(BF))
+    return jnp.concatenate(out, axis=0), [jnp.concatenate(s, axis=1) for s in sums]
+
+
+def forward_kernel(
+    length, tokens, first, s_qkv, s_out, s_gate, s_up, s_down, s_gain, cosine, low_sine, high_sine,
+    layer_out, n1_o, q_o, k_o, v_o, o_o, lse_o, x2_o, n2_o, h_o, a_o, b_o, g_qkv, g_out, g_gate, g_up, g_down, g_gain,
+    f_qkv, f_out, f_gate, f_up, f_down, f_gain,
+    tok, fst, n1, q, k, v, o, lse, x2, n2, h, ab, cos, sin_lo, sin_hi,
+    send, recv, local, fetch, store, store_ab,
+):
+    at = place()
+    tok_copy = pltpu.make_async_copy(tokens, tok, fetch.at[0])
+    tok_copy.start()
+    greet(*at)
+    shards = {QKV: s_qkv, OUT: s_out, GATE: s_gate, UP: s_up, DOWN: s_down, GAIN: s_gain}
+    fulls = {QKV: f_qkv, OUT: f_out, GATE: f_gate, UP: f_up, DOWN: f_down, GAIN: f_gain}
+    outs = {QKV: g_qkv, OUT: g_out, GATE: g_gate, UP: g_up, DOWN: g_down, GAIN: g_gain}
+    ag = {g: Gather(at, SPECS[g], shards[g], fulls[g], send, recv, local, g) for g in SPECS}
+    for g in (GAIN, QKV, OUT, GATE, UP, DOWN):
+        ag[g].tick0()
+    loads = [
+        pltpu.make_async_copy(a, b, fetch.at[i + 1])
+        for i, (a, b) in enumerate(((first, fst), (cosine, cos), (low_sine, sin_lo), (high_sine, sin_hi)))
+    ]
+    for copy in loads:
+        copy.start()
+    stores = []
+
+    def save(a, b):
+        copy = pltpu.make_async_copy(a, b, store.at[len(stores)])
+        copy.start()
+        stores.append(copy)
+
+    tok_copy.wait()
+    ag[GAIN].tick1()
+    ag[GAIN].tick2()
+    ag[QKV].tick1()
+    ag[GAIN].tick3()
+    ag[GAIN].tick4()
+    gain = jnp.concatenate([f_gain[z, y, 0:32, :] for z in range(4) for y in range(2)], axis=1).astype(F32)
+    gain_one, gain_two = gain[0:1], gain[16:17]
+    rows = tok.shape[0]
+    step = 256
+
+    def norm_one(i, _):
+        at_rows = pl.ds(pl.multiple_of(i * step, step), step)
+        t = tok[at_rows].astype(F32)
+        inverse = lax.rsqrt(jnp.mean(t * t, axis=-1, keepdims=True) + 1e-06)
+        n1[at_rows] = (t * inverse * gain_one).astype(BF)
+        return 0
+
+    lax.fori_loop(0, rows // step, norm_one, 0)
+    save(n1, n1_o)
+    ag[QKV].tick2()
+    ag[OUT].tick1()
+    ag[QKV].tick3()
+    ag[OUT].tick2()
+    ag[GATE].tick1()
+    ag[QKV].tick4()
+    save(f_qkv, g_qkv)
+    save(f_gain, g_gain)
+    for copy in loads:
+        copy.wait()
+
+    def project(z, _):
+        weights = jnp.concatenate([f_qkv[z, 0], f_qkv[z, 1]], axis=1)
+        for part in range(2):
+            at_rows = pl.ds(part * (rows // 2), rows // 2)
+            both = mm(n1[at_rows], weights, NN)
+            for y in range(2):
+                one = both[:, y * 384 : y * 384 + 384]
+                c, lo, hi = cos[at_rows], sin_lo[at_rows], sin_hi[at_rows]
+                q[2 * z + y, at_rows] = (turn(one[:, 0:128], c, lo, hi).astype(BF).astype(F32) * 0.125).astype(BF)
+                k[2 * z + y, at_rows] = turn(one[:, 128:256], c, lo, hi).astype(BF)
+                cols = pl.ds(pl.multiple_of((2 * z + y) * 128, 128), 128)
+                v[2 * z + y, at_rows] = (0.5 * one[:, 256:384] + 0.5 * fst[at_rows, cols].astype(F32)).astype(BF)
+        return 0
+
+    def attend(p, _):
+        result, sums = attend_pair(q[p], k[p], v[p], min(256, rows))
+        o[:, pl.ds(pl.multiple_of(p * 128, 128), 128)] = result
+        for head in range(2):
+            lse[p, pl.ds(head, 1)] = sums[head]
+        return 0
+
+    lax.fori_loop(0, 2, project, 0)
+    ag[OUT].tick3()
+    lax.fori_loop(2, 4, project, 0)
+    save(q, q_o)
+    save(k, k_o)
+    save(v, v_o)
+    ag[GATE].tick2()
+    ag[UP].tick1()
+    lax.fori_loop(0, 4, attend, 0)
+    ag[OUT].tick4()
+    save(f_out, g_out)
+    ag[GATE].tick3()
+    ag[UP].tick2()
+    ag[DOWN].tick1()
+    lax.fori_loop(4, 8, attend, 0)
+    save(o, o_o)
+    save(lse, lse_o)
+
+    def mix(z, _):
+        weights = jnp.concatenate([f_out[z, 0], f_out[z, 1]], axis=1)
+        cols = pl.ds(pl.multiple_of(z * 256, 256), 256)
+        x2[:, cols] = tok[:, cols].astype(F32) + mm(o[...], weights, NN)
+        return 0
+
+    lax.fori_loop(0, 4, mix, 0)
+    save(x2, x2_o)
+
+    def norm_two(i, _):
+        at_rows = pl.ds(pl.multiple_of(i * step, step), step)
+        t = x2[at_rows]
+        inverse = lax.rsqrt(jnp.mean(t * t, axis=-1, keepdims=True) + 1e-06)
+        n2[at_rows] = (t * inverse * gain_two).astype(BF)
+        return 0
+
+    lax.fori_loop(0, rows // step, norm_two, 0)
+    save(n2, n2_o)
+    ag[GATE].tick4()
+    save(f_gate, g_gate)
+    ag[UP].tick3()
+    ag[DOWN].tick2()
+    ag[UP].tick4()
+    save(f_up, g_up)
+    width = 352
+
+    def put_ab(f, slot):
+        at_h = pl.ds(pl.multiple_of(f * width, 16), width)
+        return [
+            pltpu.make_async_copy(ab.at[slot, i], target.at[at_h], store_ab.at[slot, i])
+            for i, target in enumerate((a_o, b_o))
+        ]
+
+    def hidden(f, _):
+        z, y = f // 2, f % 2
+        slot = lax.rem(f, 2)
+
+        @pl.when(f >= 2)
+        def _():
+            for copy in put_ab(f - 2, slot):
+                copy.wait()
+
+        for part in range(2):
+            span = pl.ds(part * 176, 176)
+            gate = mm(f_gate[z, y, span], n2[...], NT)
+            up = mm(f_up[z, y, span], n2[...], NT)
+            s = 1.0 / (1.0 + jnp.exp(-gate))
+            silu = gate * s
+            at_h = pl.ds(pl.multiple_of(f * width + part * 176, 16), 176)
+            h[at_h] = (silu * up).astype(BF)
+            ab[slot, 0, span] = (up * (s * (1.0 + gate * (1.0 - s)))).astype(BF)
+            ab[slot, 1, span] = silu.astype(BF)
+        for copy in put_ab(f, slot):
+            copy.start()
+        return 0
+
+    lax.fori_loop(0, 4, hidden, 0)
+    ag[DOWN].tick3()
+    lax.fori_loop(4, 8, hidden, 0)
+    save(h, h_o)
+    ag[DOWN].tick4()
+    save(f_down, g_down)
+    live = length[0]
+
+    def last(z, _):
+        weights = jnp.concatenate([f_down[z, 0], f_down[z, 1]], axis=1)
+        cols = pl.ds(pl.multiple_of(z * 256, 256), 256)
+        result = x2[:, cols] + mm(h[...], weights, TN)
+        keep = lax.broadcasted_iota(jnp.int32, (rows, 256), 0) < live
+        fst[:, cols] = jnp.where(keep, result, 0.0).astype(BF)
+        return 0
+
+    lax.fori_loop(0, 4, last, 0)
+    save(fst, layer_out)
+    for g in SPECS:
+        ag[g].finish()
+    for copy in stores:
+        copy.wait()
+    for f in (6, 7):
+        for copy in put_ab(f, f % 2):
+            copy.wait()
+
+
+def forward(length, tokens, first, shards, tables):
+    rows, width = tokens.shape
+    hidden = 8 * shards[GATE].shape[0]
+    order = (QKV, OUT, GATE, UP, DOWN, GAIN)
+    half = jax.ShapeDtypeStruct((rows, width), BF)
+    pairs = jax.ShapeDtypeStruct((8, rows, 128), BF)
+    tall = jax.ShapeDtypeStruct((hidden, rows), BF)
+    logs = jax.ShapeDtypeStruct((8, 2, rows), F32)
+    wide = jax.ShapeDtypeStruct((rows, width), F32)
+    fulls = [jax.ShapeDtypeStruct(full_shape(SPECS[g]), BF) for g in order]
+    outs = [half, half, pairs, pairs, pairs, half, logs, wide, half, tall, tall, tall] + fulls
+    anywhere = pl.BlockSpec(memory_space=pl.ANY)
+    scratch = [pltpu.VMEM(s.shape, s.dtype) for s in fulls]
+    scratch += [pltpu.VMEM(s.shape, s.dtype) for s in (half, half, half, pairs, pairs, pairs, half, logs, wide, half, tall)]
+    scratch += [pltpu.VMEM((2, 2, hidden // 8, rows), BF)]
+    scratch += [pltpu.VMEM((rows, 128), F32)] * 3
+    scratch += [
+        pltpu.SemaphoreType.DMA((6, 14)),
+        pltpu.SemaphoreType.DMA((6, 14)),
+        pltpu.SemaphoreType.DMA((6,)),
+        pltpu.SemaphoreType.DMA((5,)),
+        pltpu.SemaphoreType.DMA((len(outs),)),
+        pltpu.SemaphoreType.DMA((2, 2)),
+    ]
+    return pl.pallas_call(
+        forward_kernel,
+        out_shape=outs,
+        in_specs=[pl.BlockSpec(memory_space=pltpu.SMEM)] + [anywhere] * 11,
+        out_specs=[anywhere] * len(outs),
+        scratch_shapes=scratch,
+        compiler_params=pltpu.CompilerParams(
+            collective_id=0, has_side_effects=True, vmem_limit_bytes=63 << 20
+        ),
+        name="forward",
+    )(length, tokens, first, *[shards[g] for g in order], *tables)
+
+
+def rope_tables(rows):
+    position = np.arange(rows, dtype=np.float32)[:, None]
+    frequency = np.float32(10000.0) ** (-np.arange(32, dtype=np.float32) * np.float32(2.0) / np.float32(64))
+    angle = (position * frequency[None, :]).astype(np.float32)
+    cosine, sine, zero = np.cos(angle), np.sin(angle), np.zeros_like(angle)
+    join = lambda parts: np.concatenate(parts, axis=1).astype(np.float32)
+    return join([cosine] * 4), join([-sine, zero] * 2), join([zero, sine] * 2)
+
+
+def on_slice(
+    tokens, first_values, lengths, cotangent, w_query, w_key, w_value, w_out, w_gate, w_up, w_down, norm_one, norm_two,
+):
+    rows, width = tokens.shape
+    gains = jnp.concatenate([jnp.broadcast_to(g[None], (16, 128)) for g in (norm_one, norm_two)], axis=0)
+    shards = {
+        QKV: jnp.concatenate([w_query, w_key, w_value], axis=1),
+        OUT: w_out,
+        GATE: w_gate.T,
+        UP: w_up.T,
+        DOWN: w_down,
+        GAIN: gains,
+    }
+    tables = [jnp.asarray(t) for t in rope_tables(rows)]
+    (
+        layer_out, n1, q, k, v, o, lse, x2, n2, h, a, b, g_qkv, g_out, g_gate, g_up, g_down, g_gain,
+    ) = forward(lengths, tokens, first_values, shards, tables)
+    g_qkv = g_qkv.reshape(8, 1024, 384)
+    whole = lambda w: jnp.moveaxis(w, 0, 1).reshape(w.shape[1], -1)
+    query_w, key_w, value_w = (whole(g_qkv[:, :, i * 128 : i * 128 + 128]) for i in range(3))
+    out_w, down_w = whole(g_out.reshape(8, 1024, 128)), whole(g_down.reshape(8, 2816, 128))
+    gate_t, up_t = g_gate.reshape(2816, 1024), g_up.reshape(2816, 1024)
+    gain_one_wide = g_gain.reshape(8, 128, 128)[:, 0].reshape(-1).astype(jnp.float32)
+    gain_two_wide = g_gain.reshape(8, 128, 128)[:, 16].reshape(-1).astype(jnp.float32)
+    positions = jnp.arange(rows, dtype=jnp.int32)
+    keep_rows = (positions[None, :] < lengths[:, None]).astype(jnp.float32).reshape(rows, 1)
+    heads = lambda t: jnp.moveaxis(t, 0, 1).reshape(rows, HEADS, HEAD_DIM)
+    query_rot, key_rot, values_mix = heads(q * 8), heads(k), heads(v)
+    logsum = jnp.moveaxis(lse.reshape(16, 2, 512), 1, 0)
+    tokens_wide = tokens.astype(jnp.float32)
+    grad_top = cotangent.astype(jnp.float32) * keep_rows
+    grad_ffn = grad_top.astype(jnp.bfloat16)
+    down_sum = jnp.einsum("fr,rd->fd", h, grad_ffn, preferred_element_type=jnp.float32)
+    grad_hidden = jnp.einsum("rd,fd->fr", grad_ffn, down_w, preferred_element_type=jnp.float32)
+    grad_gate_low = (grad_hidden * a).astype(jnp.bfloat16)
+    grad_up_low = (grad_hidden * b).astype(jnp.bfloat16)
+    gate_sum = jnp.einsum("rd,fr->df", n2, grad_gate_low, preferred_element_type=jnp.float32)
+    up_sum = jnp.einsum("rd,fr->df", n2, grad_up_low, preferred_element_type=jnp.float32)
+    grad_second = jnp.einsum("fr,fd->rd", grad_gate_low, gate_t, preferred_element_type=jnp.float32) + jnp.einsum(
+        "fr,fd->rd", grad_up_low, up_t, preferred_element_type=jnp.float32
+    )
+    _, norm_two_back = jax.vjp(rms_norm, x2, gain_two_wide)
+    grad_mixed_norm, gain_two_sum = norm_two_back(grad_second)
+    grad_mixed = grad_top + grad_mixed_norm
+    grad_branch = grad_mixed.astype(jnp.bfloat16)
+    out_sum = jnp.einsum("rd,re->de", o, grad_branch, preferred_element_type=jnp.float32)
+    grad_attended = jnp.einsum("re,de->rd", grad_branch, out_w, preferred_element_type=jnp.float32).astype(jnp.bfloat16)
+    query_back, key_back, value_back = attend_backward(
+        query_rot, key_rot, values_mix, grad_attended.reshape(rows, HEADS, HEAD_DIM), logsum, 512
+    )
+    rope_rows = partial(rotate, positions=positions)
+    _, rope_back = jax.vjp(rope_rows, query_back)
+    grad_query_low = rope_back(query_back)[0].reshape(rows, 1024).astype(jnp.bfloat16)
+    grad_key_low = rope_back(key_back)[0].reshape(rows, 1024).astype(jnp.bfloat16)
+    value_mix_grad = value_back.reshape(rows, 1024)
+    first_grad = 0.5 * value_mix_grad
+    grad_value_low = (0.5 * value_mix_grad).astype(jnp.bfloat16)
+    dot = lambda e, s, t: jnp.einsum(e, s, t, preferred_element_type=jnp.float32)
+    query_sum, key_sum, value_sum = (dot("rd,re->de", n1, g) for g in (grad_query_low, grad_key_low, grad_value_low))
+    grad_normed = (
+        dot("re,de->rd", grad_query_low, query_w)
+        + dot("re,de->rd", grad_key_low, key_w)
+        + dot("re,de->rd", grad_value_low, value_w)
+    )
+    _, norm_one_back = jax.vjp(rms_norm, tokens_wide, gain_one_wide)
+    grad_tokens_norm, gain_one_sum = norm_one_back(grad_normed)
+    input_grad = grad_mixed + grad_tokens_norm
+
+    def reduce(total):
+        total = lax.psum_scatter(total, "dp", scatter_dimension=0, tiled=True)
+        return lax.psum_scatter(total, "fsdp", scatter_dimension=1, tiled=True)
+
+    sums = (query_sum, key_sum, value_sum, out_sum, gate_sum, up_sum, down_sum)
+    sums = [reduce(s) for s in sums]
+    gain_grads = lax.psum(
+        [lax.psum_scatter(g, "fsdp", scatter_dimension=0, tiled=True) for g in (gain_one_sum, gain_two_sum)], "dp"
+    )
+    return (layer_out, input_grad, first_grad, *sums, *gain_grads)
+
+
 def solution(mesh):
     in_specs = (
         P(("dp", "fsdp"), None),
@@ -363,6 +843,7 @@
         P("fsdp"),
         P("fsdp"),
     )
+    on_device = on_slice if dict(mesh.shape) == {"dp": 4, "fsdp": 8} else on_device_general
     return jax.shard_map(
         on_device, mesh=mesh, in_specs=in_specs, out_specs=out_specs, check_vma=False
     )

time: 2030 us -> 1670 us (0.82)
  waiting for transfers between devices: 1060 us -> 825 us
  blocking collectives: 186 us -> 28 us
  Pallas kernels: 0 us -> 152 us
  matrix products: 554 us -> 448 us
  other arithmetic: 61.9 us -> 30.9 us
    reduce_scatter x14 -> x12, waiting for transfers between devices: 1010 us -> 674 us  [the longest x7 398 us: reduce(): total = lax.psum_scatter(total, 'dp', scatter_dimension=0, tiled=True)]
    all_gather x6 -> x0, blocking collectives: 160 us -> none  [the longest x1 32.5 us: on_device(): lax.all_gather(w_key, 'fsdp', axis=1, tiled=True)]
    pallas_call x0 -> x1, Pallas kernels: none -> 152 us  [forward(): pl.pallas_call(forward_kernel, out_shape=outs, in_specs=[pl.BlockSpec(mem...]
    unnamed x24 -> x16, waiting for transfers between devices: 3.7 us -> 151 us
    dot_general x23 -> x14, matrix products: 206 us -> 119 us  [the longest x6 27.9 us: on_slice(): jnp.einsum(e, s, t, preferred_element_type=jnp.float32)]
    all_gather x10 -> x0, waiting for transfers between devices: 45.9 us -> none  [the longest x1 16.4 us: on_device(): lax.all_gather(value_part, 'dp', axis=0, tiled=True)]
    reduce_sum x2 -> x0, other arithmetic: 32.9 us -> none  [one_block(): row_total = jnp.sum(exponent, axis=-1, keepdims=True)]
    dot_general x4 -> x2, matrix products: 57.4 us -> 35 us  [masked_scores(): jnp.einsum('qhd,khd->hqk', query_blk, keys_seq, preferred_element_type=jn...]
  transfers between devices with their start and end apart: 24 -> 14, of which waited for: 16 -> 12; matrix products, arithmetic and copies ran while one was open for 13% -> 7% of each run, Pallas kernels for 0% -> 0%
where the time goes in v1:
time: 1670 us; the launch traced here: 1660 us
  waiting for transfers between devices  825 us (49%)
  matrix products  448 us (27%)
  local copies, waits for them, and re-layouts  155 us (9%)
  Pallas kernels  152 us (9%)
  other arithmetic  30.9 us (2%)
  blocking collectives  28 us (2%)
    reduce_scatter x7, waiting for transfers between devices, reduce(): total = lax.psum_scatter(total, 'dp', scatter_dimension=0, tiled=True)  398 us
    reduce_scatter x5, waiting for transfers between devices, reduce(): return lax.psum_scatter(total, 'fsdp', scatter_dimension=1, tiled=True)  275 us
    pallas_call x1, Pallas kernels, forward(): pl.pallas_call(forward_kernel, out_shape=outs, in_specs=[pl.BlockSpec(mem...  152 us
    unnamed x16, waiting for transfers between devices  151 us
    dot_general x2, matrix products, one_block(): jnp.einsum('hqk,qhd->khd', grad_scores, query_blk, preferred_element_type...  114 us
    dot_general x2, matrix products, one_block(): jnp.einsum('hqk,khd->qhd', grad_scores, keys_seq, preferred_element_type=...  108 us
    dynamic_update_slice x4, local copies, waits for them, and re-layouts, attend_backward(): lax.scan(one_block, (zeros_seq, zeros_seq), jnp.arange(block_count, dtype...  83.6 us
    dot_general x2, matrix products, one_block(): jnp.einsum('hqk,qhd->khd', prob_low, grad_blk, preferred_element_type=jnp...  36.3 us
  transfers between devices with their start and end apart: 14, of which 12 were waited for; matrix products, arithmetic and copies ran while one was open for 7% of the time, Pallas kernels for 0%

profile of v1, /device:TPU:0, one launch (start us, length us, event | category | flops | bytes accessed | tf_op | source)
XLA Modules:
  0.0 1660.1 jit_solution(2618815672020408038)
XLA Ops:
  12.5 151.5 %forward.1 = (bf16[1024,1024]{1,0:T(8,128)(2,1)}, bf16[1024,1024]{1,0:T(8,128)(2,1)}, bf16[8,1024,128]{2,1,0:T(8,128)(2,1)}, bf16[8,1024,128]{2,1,0:T(8,128)(2,1...) custom-call(s32[1]{0:T(128)} %copy.95.length, ...), custom_call_target="tpu_custom_call" | custom-call | tf_op jit(solution)/shard_map/forward/pallas_call | solution.py:714
  164.1 2.5 multiply_reduce_fusion.3
  168.0 8.4 copy.45
  176.4 12.0 fusion.73
  188.4 12.1 fusion.80
  200.5 14.2 multiply_reduce_fusion.1
  216.5 2.6 copy.46
  219.1 4.1 copy.47
  223.2 3.9 copy.49
  227.1 2.6 copy.50
  229.8 5.0 fusion.59
  234.8 3.8 convolution_convert_fusion
  238.6 420.0 %while.15 = (s32[]{:T(128)}, f32[1024,16,64]{0,2,1:T(8,128)}, f32[1024,16,64]{0,2,1:T(8,128)}, f32[2,512,16,64]{1,0,3,2:T(2,128)}, s32[2]{0:T(128)S(1)}, /*index...) while((s32[]{:T(128)}, f32[1024,16,64]{0,2,1:T(8,128)}, ...), condition=%wide.region_4.0_spmd.clone, body=%wide.region_2.4_spmd.clone.sunk | while | flops 5591550464 | bytes 342561024 | solution.py:95
  240.0 17.5 %fusion.132 = f32[16,512,1024]{2,1,0:T(8,128)} fusion(bf16[1024,16,64]{0,2,1:T(8,128)(2,1)} %get-tuple-element.321, bf16[1024,16,64]{0,2,1:T(8,128)(2,1)} %get-tuple-element.320, s32[]{:T(128)S(6)} %select_n.56), kind=kOutput, calls=%fused_computation.23.clone.1 | convolution fusion | flops 1073741824 | bytes 36700164 | tf_op jit(solution)/shard_map/while/body/eval_jaxpr/qhd,khd->hqk/dot_general | solution.py:78
  257.6 17.5 %fusion.133 = f32[16,512,1024]{2,1,0:T(8,128)} fusion(bf16[1024,16,64]{0,2,1:T(8,128)(2,1)} %get-tuple-element.318, bf16[1024,16,64]{0,2,1:T(8,128)(2,1)} %get-tuple-element.317, s32[]{:T(128)S(6)} %select_n.56), kind=kOutput, calls=%fused_computation.26.clone.1 | convolution fusion | flops 1073741824 | bytes 36700164 | tf_op jit(solution)/shard_map/while/body/eval_jaxpr/qhd,khd->hqk/dot_general | solution.py:39
  277.4 56.9 %bitcast_add_fusion.4 = f32[1024,16,64]{0,2,1:T(8,128)} fusion(f32[1024,16,64]{0,2,1:T(8,128)} %get-tuple-element.298, f32[16,512,1024]{2,1,0:T(8,128)} %fusion.132, f32[16,512,1024]{2,1,0:T(8,128)} %fusion.133, f32[16,512]{1,0:T(8,128)S(1)} %dynamic-slice_bitcast_fusion.2, pred[512,1024]{1,0:T(8,128)(4,1)S(1)} %iota_compare_fusion.3, ...), kind=kOutput, calls=%fused_computation.19.clone.1 | convolution fusion | flops 1168122880 | bytes 144769024 | tf_op jit(solution)/shard_map/while/body/eval_jaxpr/hqk,qhd->khd/dot_general | solution.py:86
  334.3 17.6 %bitcast_add_fusion.5 = f32[1024,16,64]{0,2,1:T(8,128)} fusion(f32[1024,16,64]{0,2,1:T(8,128)} %get-tuple-element.299, f32[16,512,1024]{2,1,0:T(8,128)} %fusion.133, f32[16,512]{1,0:T(8,128)S(1)} %dynamic-slice_bitcast_fusion.2, pred[512,1024]{1,0:T(8,128)(4,1)S(1)} %iota_compare_fusion.3, pred[]{:T(512)S(6)} %compare.7, ...), kind=kOutput, calls=%fused_computation.18.clone.1 | convolution fusion | flops 1109393408 | bytes 43548676 | tf_op jit(solution)/shard_map/while/body/eval_jaxpr/hqk,qhd->khd/dot_general | solution.py:89
  351.9 54.0 %fusion.134 = f32[1,512,16,64]{1,3,2,0:T(8,128)} fusion(bf16[1024,16,64]{0,2,1:T(8,128)(2,1)} %get-tuple-element.318, f32[16,512,1024]{2,1,0:T(8,128)} %fusion.132, f32[16,512,1024]{2,1,0:T(8,128)} %fusion.133, f32[16,512]{1,0:T(8,128)S(1)} %dynamic-slice_bitcast_fusion.2, pred[512,1024]{1,0:T(8,128)(4,1)S(1)} %iota_compare_fusion.3), kind=kOutput, calls=%fused_computation.21.clone.1 | convolution fusion | flops 1166025728 | bytes 71860224 | tf_op jit(solution)/shard_map/while/body/eval_jaxpr/hqk,khd->qhd/dot_general | solution.py:83
  405.9 3.7 copy.80
  409.6 38.0 %dynamic_update_slice.6 = f32[2,512,16,64]{1,0,3,2:T(2,128)} dynamic-update-slice(f32[2,512,16,64]{1,0,3,2:T(2,128)} %get-tuple-element.300, f32[1,512,16,64]{1,0,3,2:T(1,128)S(1)} %copy.80, s32[]{:T(128)S(6)} %copy.86, s32[]{:T(128)} %constant.15.clone.1..sunk, s32[]{:T(128)} %constant.15.clone.1..sunk, s32[]{:T(128)} %constant.15.clone.1..sunk) | dynamic-update-slice | bytes 4194308 | tf_op jit(solution)/shard_map/while/body/jit(dynamic_update_index_in_dim)/dynamic_update_slice | solution.py:95
  448.9 17.5 %fusion.132 = f32[16,512,1024]{2,1,0:T(8,128)} fusion(bf16[1024,16,64]{0,2,1:T(8,128)(2,1)} %get-tuple-element.321, bf16[1024,16,64]{0,2,1:T(8,128)(2,1)} %get-tuple-element.320, s32[]{:T(128)S(6)} %select_n.56), kind=kOutput, calls=%fused_computation.23.clone.1 | convolution fusion | flops 1073741824 | bytes 36700164 | tf_op jit(solution)/shard_map/while/body/eval_jaxpr/qhd,khd->hqk/dot_general | solution.py:78
  466.4 17.5 %fusion.133 = f32[16,512,1024]{2,1,0:T(8,128)} fusion(bf16[1024,16,64]{0,2,1:T(8,128)(2,1)} %get-tuple-element.318, bf16[1024,16,64]{0,2,1:T(8,128)(2,1)} %get-tuple-element.317, s32[]{:T(128)S(6)} %select_n.56), kind=kOutput, calls=%fused_computation.26.clone.1 | convolution fusion | flops 1073741824 | bytes 36700164 | tf_op jit(solution)/shard_map/while/body/eval_jaxpr/qhd,khd->hqk/dot_general | solution.py:39
  486.3 57.4 %bitcast_add_fusion.4 = f32[1024,16,64]{0,2,1:T(8,128)} fusion(f32[1024,16,64]{0,2,1:T(8,128)} %get-tuple-element.298, f32[16,512,1024]{2,1,0:T(8,128)} %fusion.132, f32[16,512,1024]{2,1,0:T(8,128)} %fusion.133, f32[16,512]{1,0:T(8,128)S(1)} %dynamic-slice_bitcast_fusion.2, pred[512,1024]{1,0:T(8,128)(4,1)S(1)} %iota_compare_fusion.3, ...), kind=kOutput, calls=%fused_computation.19.clone.1 | convolution fusion | flops 1168122880 | bytes 144769024 | tf_op jit(solution)/shard_map/while/body/eval_jaxpr/hqk,qhd->khd/dot_general | solution.py:86
  543.7 18.8 %bitcast_add_fusion.5 = f32[1024,16,64]{0,2,1:T(8,128)} fusion(f32[1024,16,64]{0,2,1:T(8,128)} %get-tuple-element.299, f32[16,512,1024]{2,1,0:T(8,128)} %fusion.133, f32[16,512]{1,0:T(8,128)S(1)} %dynamic-slice_bitcast_fusion.2, pred[512,1024]{1,0:T(8,128)(4,1)S(1)} %iota_compare_fusion.3, pred[]{:T(512)S(6)} %compare.7, ...), kind=kOutput, calls=%fused_computation.18.clone.1 | convolution fusion | flops 1109393408 | bytes 43548676 | tf_op jit(solution)/shard_map/while/body/eval_jaxpr/hqk,qhd->khd/dot_general | solution.py:89
  562.5 54.0 %fusion.134 = f32[1,512,16,64]{1,3,2,0:T(8,128)} fusion(bf16[1024,16,64]{0,2,1:T(8,128)(2,1)} %get-tuple-element.318, f32[16,512,1024]{2,1,0:T(8,128)} %fusion.132, f32[16,512,1024]{2,1,0:T(8,128)} %fusion.133, f32[16,512]{1,0:T(8,128)S(1)} %dynamic-slice_bitcast_fusion.2, pred[512,1024]{1,0:T(8,128)(4,1)S(1)} %iota_compare_fusion.3), kind=kOutput, calls=%fused_computation.21.clone.1 | convolution fusion | flops 1166025728 | bytes 71860224 | tf_op jit(solution)/shard_map/while/body/eval_jaxpr/hqk,khd->qhd/dot_general | solution.py:83
  616.5 3.7 copy.80
  620.2 38.0 %dynamic_update_slice.6 = f32[2,512,16,64]{1,0,3,2:T(2,128)} dynamic-update-slice(f32[2,512,16,64]{1,0,3,2:T(2,128)} %get-tuple-element.300, f32[1,512,16,64]{1,0,3,2:T(1,128)S(1)} %copy.80, s32[]{:T(128)S(6)} %copy.86, s32[]{:T(128)} %constant.15.clone.1..sunk, s32[]{:T(128)} %constant.15.clone.1..sunk, s32[]{:T(128)} %constant.15.clone.1..sunk) | dynamic-update-slice | bytes 4194308 | tf_op jit(solution)/shard_map/while/body/jit(dynamic_update_index_in_dim)/dynamic_update_slice | solution.py:95
  658.7 6.6 reshape.247
  665.8 4.7 multiply_add_fusion.1
  672.6 4.4 fusion.85
  677.0 5.9 fusion.86
  683.0 4.4 broadcast_multiply_fusion
  687.4 2.1 copy-done.1
  689.5 4.7 fusion.66
  696.0 6.7 fusion.68
  704.5 15.2 fusion.79
  719.8 15.2 fusion.81
  736.5 12.3 fusion.71
  749.7 27.6 %reduce-scatter.23.cloned.1.call-done = f32[256,1024]{1,0:T(8,128)} async-done(((f32[1024,1024]{1,0:T(8,128)}), f32[256,1024]{1,0:T(8,128)}) %reduce-scatter.23.cloned.1.call-update) | async-done | bytes 1048592 | tf_op jit(solution)/shard_map/reduce_scatter | solution.py:805
  777.3 47.0 %reduce-scatter.27.cloned.1.call-done = f32[256,1024]{1,0:T(8,128)} async-done(((f32[1024,1024]{1,0:T(8,128)}), f32[256,1024]{1,0:T(8,128)}) %reduce-scatter.27.cloned.1.call-update) | async-done | bytes 1048592 | tf_op jit(solution)/shard_map/reduce_scatter | solution.py:805
  824.4 47.0 %reduce-scatter.31.cloned.1.call-done = f32[256,1024]{1,0:T(8,128)} async-done(((f32[1024,1024]{1,0:T(8,128)}), f32[256,1024]{1,0:T(8,128)}) %reduce-scatter.31.cloned.1.call-update) | async-done | bytes 1048592 | tf_op jit(solution)/shard_map/reduce_scatter | solution.py:805
  871.4 94.6 %reduce-scatter.35.cloned.1.call-done = f32[256,2816]{1,0:T(8,128)} async-done(((f32[1024,2816]{1,0:T(8,128)}), f32[256,2816]{1,0:T(8,128)}) %reduce-scatter.35.cloned.1.call-update) | async-done | bytes 2883600 | tf_op jit(solution)/shard_map/reduce_scatter | solution.py:805
  966.0 3.4 copy.58
  969.5 91.2 %reduce-scatter.37.cloned.1.call-done = f32[256,2816]{1,0:T(8,128)} async-done(((f32[1024,2816]{1,0:T(8,128)}), f32[256,2816]{1,0:T(8,128)}) %reduce-scatter.37.cloned.1.call-update) | async-done | bytes 2883600 | tf_op jit(solution)/shard_map/reduce_scatter | solution.py:805
  1060.7 3.4 copy.60
  1064.4 91.1 %reduce-scatter.39.cloned.1.call-done = f32[704,1024]{1,0:T(8,128)} async-done(((f32[2816,1024]{1,0:T(8,128)}), f32[704,1024]{1,0:T(8,128)}) %reduce-scatter.39.cloned.1.call-update) | async-done | bytes 2883600 | tf_op jit(solution)/shard_map/reduce_scatter | solution.py:805
  1155.5 5.3 copy.55
  1160.9 5.4 fusion.82
  1166.3 2.6 copy.66
  1168.9 4.1 copy.64
  1172.9 3.9 copy.65
  1178.6 4.9 fusion.83
  1183.5 2.4 fusion.84
  1186.0 5.6 fusion.64
  1191.6 21.6 %all-reduce.6 = (f32[1024]{0:T(1024)S(1)}, f32[1024]{0:T(1024)S(1)}) all-reduce(f32[1024]{0:T(1024)S(1)} %get-tuple-element.176, f32[1024]{0:T(1024)S(1)} %copy-done.19), channel_id=16, replica_groups=mesh['dp'=4,'fsdp'=8] {'fsdp'}, use_global_device_ids=true, to_apply=%region_22.23.clone | all-reduce | flops 2048 | bytes 16384
  1213.4 6.3 all-reduce.7
  1219.7 5.4 fusion.60
  1225.1 65.8 %reduce-scatter.25.cloned.1.call-done = f32[256,128]{1,0:T(8,128)} async-done(((f32[256,1024]{1,0:T(8,128)}), f32[256,128]{1,0:T(8,128)}) %reduce-scatter.25.cloned.1.call-update) | async-done | bytes 131088 | tf_op jit(solution)/shard_map/reduce_scatter | solution.py:806
  1290.9 66.9 %reduce-scatter.29.cloned.1.call-done = f32[256,128]{1,0:T(8,128)} async-done(((f32[256,1024]{1,0:T(8,128)}), f32[256,128]{1,0:T(8,128)}) %reduce-scatter.29.cloned.1.call-update) | async-done | bytes 131088 | tf_op jit(solution)/shard_map/reduce_scatter | solution.py:806
  1357.8 67.2 %reduce-scatter.33.cloned.1.call-done = f32[256,128]{1,0:T(8,128)} async-done(((f32[256,1024]{1,0:T(8,128)}), f32[256,128]{1,0:T(8,128)}) %reduce-scatter.33.cloned.1.call-update) | async-done | bytes 131088 | tf_op jit(solution)/shard_map/reduce_scatter | solution.py:806
  1425.0 74.8 %reduce-scatter.43.cloned.1.call-done = f32[352,256]{1,0:T(8,128)} async-done(((f32[2816,256]{1,0:T(8,128)}), f32[352,256]{1,0:T(8,128)}) %reduce-scatter.43.cloned.1.call-update) | async-done | bytes 360464
  1499.8 75.1 %reduce-scatter.45.cloned.1.call-done = f32[352,256]{1,0:T(8,128)} async-done(((f32[2816,256]{1,0:T(8,128)}), f32[352,256]{1,0:T(8,128)}) %reduce-scatter.45.cloned.1.call-update) | async-done | bytes 360464
  1574.9 75.4 %reduce-scatter.41.cloned.1.call-done = f32[704,128]{1,0:T(8,128)} async-done(((f32[704,1024]{1,0:T(8,128)}), f32[704,128]{1,0:T(8,128)}) %reduce-scatter.41.cloned.1.call-update) | async-done | bytes 360464 | tf_op jit(solution)/shard_map/reduce_scatter | solution.py:806
  1650.3 3.1 copy.96
  (114 shorter events, 20.3 us)
Async XLA Ops:
  7.2 741.8 %reduce-scatter.19.cloned.1.call-start = ((), (), s32[]{:S(2)}) async-start(), calls=%async_computation.14 | async-start | bytes 5242880 | tf_op jit(solution)/shard_map/reduce_scatter | solution.py:805
  168.0 8.4 copy-start.9
  176.3 53.4 %copy-start.15 = (f32[1024]{0:T(1024)}, f32[1024]{0:T(1024)S(1)}, u32[]{:S(2)}) copy-start(f32[1024]{0:T(1024)S(1)} %fusion.75) | copy-start | bytes 12292
  188.4 12.1 copy-start.2
  216.4 6.7 copy-start.14
  219.1 8.1 copy-start.5
  229.8 5.0 copy-start.8
  234.8 3.8 copy-start.3
  658.7 6.6 copy-start.17
  658.7 6.6 copy-start.20
  670.5 2.0 copy-start.23
  671.2 1.3 copy-start.13
  671.2 5.8 copy-start.11
  677.0 100.3 %reduce-scatter.23.cloned.1.call-start = ((), (), s32[]{:S(2)}) async-start(), calls=%async_computation.16 | async-start | bytes 5242880 | tf_op jit(solution)/shard_map/reduce_scatter | solution.py:805
  683.0 141.3 %reduce-scatter.27.cloned.1.call-start = ((), (), s32[]{:S(2)}) async-start(), calls=%async_computation.18 | async-start | bytes 5242880 | tf_op jit(solution)/shard_map/reduce_scatter | solution.py:805
  683.0 6.4 copy-start.24
  687.4 2.1 copy-start.1
  694.1 1.9 copy-start.22
  694.2 177.2 %reduce-scatter.31.cloned.1.call-start = ((), (), s32[]{:S(2)}) async-start(), calls=%async_computation.20 | async-start | bytes 5242880 | tf_op jit(solution)/shard_map/reduce_scatter | solution.py:805
  702.7 1.8 copy-start.21
  702.8 263.3 %reduce-scatter.35.cloned.1.call-start = ((), (), s32[]{:S(2)}) async-start(), calls=%async_computation.22 | async-start | bytes 14417920 | tf_op jit(solution)/shard_map/reduce_scatter | solution.py:805
  719.7 341.0 %reduce-scatter.37.cloned.1.call-start = ((), (), s32[]{:S(2)}) async-start(), calls=%async_computation.23 | async-start | bytes 14417920 | tf_op jit(solution)/shard_map/reduce_scatter | solution.py:805
  734.9 1.6 copy-start.10
  734.9 1.6 copy-start.16
  735.0 420.6 %reduce-scatter.39.cloned.1.call-start = ((), (), s32[]{:S(2)}) async-start(), calls=%async_computation.24 | async-start | bytes 14417920 | tf_op jit(solution)/shard_map/reduce_scatter | solution.py:805
  748.9 476.3 %reduce-scatter.21.cloned.1.call-start = ((), (), s32[]{:S(2)}) async-start(), calls=%async_computation.15 | async-start | bytes 1179648 | tf_op jit(solution)/shard_map/reduce_scatter | solution.py:806
  749.6 541.3 %reduce-scatter.25.cloned.1.call-start = ((), (), s32[]{:S(2)}) async-start(), calls=%async_computation.17 | async-start | bytes 1179648 | tf_op jit(solution)/shard_map/reduce_scatter | solution.py:806
  777.3 580.5 %reduce-scatter.29.cloned.1.call-start = ((), (), s32[]{:S(2)}) async-start(), calls=%async_computation.19 | async-start | bytes 1179648 | tf_op jit(solution)/shard_map/reduce_scatter | solution.py:806
  824.3 600.7 %reduce-scatter.33.cloned.1.call-start = ((), (), s32[]{:S(2)}) async-start(), calls=%async_computation.21 | async-start | bytes 1179648 | tf_op jit(solution)/shard_map/reduce_scatter | solution.py:806
  871.4 628.4 %reduce-scatter.43.cloned.1.call-start = ((), (), s32[]{:S(2)}) async-start(), calls=%async_computation.26 | async-start | bytes 3244032
  969.5 605.4 %reduce-scatter.45.cloned.1.call-start = ((), (), s32[]{:S(2)}) async-start(), calls=%async_computation.27 | async-start | bytes 3244032
  1064.2 586.1 %reduce-scatter.41.cloned.1.call-start = ((), (), s32[]{:S(2)}) async-start(), calls=%async_computation.25 | async-start | bytes 3244032 | tf_op jit(solution)/shard_map/reduce_scatter | solution.py:806
  1168.8 8.0 copy-start.25
  1168.8 9.2 copy-start
  1178.6 4.9 copy-start.7
  1178.6 4.9 copy-start.12
  1183.5 2.5 copy-start.4
  1183.5 2.5 copy-start.6
  1183.5 2.5 copy-start.18
  1186.0 5.6 copy-start.19
Sparse Core Ops, SparseCore 0:
  677.1 52.8 reduce-scatter.18
  732.7 44.5 reduce-scatter.22
  779.8 44.4 reduce-scatter.26
  826.8 44.4 reduce-scatter.30
  873.8 92.1 reduce-scatter.34
  968.5 92.1 reduce-scatter.36
  1063.3 92.1 reduce-scatter.38
  1159.5 63.9 reduce-scatter.20
  1227.9 62.9 reduce-scatter.24
  1294.8 62.9 reduce-scatter.28
  1362.2 62.8 reduce-scatter.32
  1429.0 70.7 reduce-scatter.42
  1503.9 70.9 reduce-scatter.44
  1578.9 71.3 reduce-scatter.40
